TPU v7x, 32 devices: a whole 2x2x4 slice. The times are simulated.
32 devices in a mesh: cases: 2 (over y), tm: 4 (over z), region: 4 (over x, core).
Axes of the slice: x: 2, y: 2, z: 4, core: 2. Of those that a mesh axis runs over, the one named last changes fastest.
Arguments:
- former_estimate: float32 [384, 32, 128], P(('cases', 'tm'), 'region'), parts along dimension 0, may hold values from -6 to 6
- excitation: bfloat16 [384, 32, 128], P(('cases', 'tm'), 'region'), parts along dimension 0, may hold values from -6 to 6
- susceptance_maps: bfloat16 [32, 4, 128, 128], P('region'), may hold values from -0.125 to 0.125
- linked_partner_target: int32 [32, 4], P('region'), may hold values from 0 to 31, as said below
- attenuation: float32 [32, 64], P('region'), may hold values from 0.0002 to 0.03
- revolution_angle: float32 [32, 64], P('region'), may hold values from -0.6 to 0.6
- saturated_flag: int32 [64, 64], P(('cases', 'region')), parts along dimension 0, may hold values 0 or 1
- gain_surge: float32 [384], P(('cases', 'tm')), parts along dimension 0, may hold values from 0.25 to 1
Outputs:
- waveform: float32 [384, 32, 128], P(('cases', 'tm'), 'region'), parts along dimension 0
There are 2 independent parts, one for each index of `cases`. A program takes and returns all parts, laid end to end along the dimension named above; an argument that names none is the same for every part. Nothing has to cross between parts.
Inputs may be any that keep to these rules, and one draw needn't show every extreme that they name: `linked_partner_target`: block row b lies in region g = b // 8. Its column 0 is b itself, column 1 a block of region g, column 2 one of the last 4 blocks of region g - 1 and column 3 one of the first 4 blocks of region g + 1, regions counted around a cycle of 32 // 8.
All inputs are finite; a program needn't handle non-finite values. No bound on the sum of `saturated_flag` on one device may be relied on, other than what follows from the above.
Results may differ from a plain program's by a relative error of at most 0.0017.
Values may be sent and summed in bfloat16 or wider, within the bound.
A program may use at most 64 MiB of HBM per device.

v0:
```python
import jax
import jax.numpy as jnp
from jax import lax
from jax.sharding import PartitionSpec as P

BND = 4
SWEEPS = 3
clip_level = 0.5


def with_halo(block, sides, width):
    for axis, dim in sides:
        count = lax.axis_size(axis)
        forward = [(i, i + 1) for i in range(count - 1)]
        forward.append((count - 1, 0))
        backward = [(target, source) for source, target in forward]
        low = lax.ppermute(
            lax.slice_in_dim(block, block.shape[dim] - width, None, axis=dim), axis, forward
        )
        high = lax.ppermute(lax.slice_in_dim(block, 0, width, axis=dim), axis, backward)
        block = jnp.concatenate([low, block, high], axis=dim)
    return block


def complex_mul(first, second):
    half = first.shape[-1] // 2
    first_re, first_im = (first[..., :half], first[..., half:])
    second_re, second_im = (second[..., :half], second[..., half:])
    return jnp.concatenate(
        [first_re * second_re - first_im * second_im, first_re * second_im + first_im * second_re],
        axis=-1,
    )


def combine(early, late):
    return (complex_mul(late[0], early[0]), complex_mul(late[0], early[1]) + late[1])


def bus_terms(attenuation, revolution_angle):
    modulus = jnp.exp(-attenuation)
    cosine = modulus * jnp.cos(revolution_angle)
    sine = modulus * jnp.sin(revolution_angle)
    argument_spin = jnp.concatenate([cosine, sine], axis=-1)
    input_gain = jnp.sqrt((1.0 - cosine) ** 2 + sine**2)
    return (argument_spin, jnp.concatenate([input_gain, input_gain], axis=-1))


def limit_current(current, saturated_flag):
    half = current.shape[-1] // 2
    square = current[..., :half] ** 2 + current[..., half:] ** 2
    scaling_factor = jnp.where(
        saturated_flag == 1, clip_level / jnp.sqrt(clip_level**2 + square), 1.0
    )
    return current * jnp.concatenate([scaling_factor, scaling_factor], axis=-1)


def periodic_end(total_a, total_b):
    half = total_a.shape[-1] // 2
    denom_re = 1.0 - total_a[..., :half]
    denom_im = -total_a[..., half:]
    square = denom_re**2 + denom_im**2
    conjugate = jnp.concatenate([denom_re / square, -denom_im / square], axis=-1)
    return complex_mul(total_b, conjugate)


def local(
    former_estimate,
    excitation,
    susceptance_maps,
    linked_partner_target,
    attenuation,
    revolution_angle,
    saturated_flag,
    gain_surge,
):
    blocks = former_estimate.shape[1]
    buses = attenuation.shape[1]
    argument_spin, input_gain = bus_terms(attenuation, revolution_angle)
    incremental_spin = gain_surge[:, None, None] * argument_spin[None]
    drive_base = excitation.astype(jnp.float32)
    region_index = lax.axis_index("region")
    network = blocks * lax.axis_size("region")
    local_col = (linked_partner_target - region_index * blocks) % network
    local_col = jnp.where(local_col >= network - BND, local_col - network, local_col) + BND
    unit = jnp.concatenate(
        [jnp.ones((blocks, buses), jnp.float32), jnp.zeros((blocks, buses), jnp.float32)], axis=-1
    )
    nothing = jnp.zeros((blocks, 2 * buses), jnp.float32)
    wave = former_estimate
    for sweep_index in range(SWEEPS):
        rounded = wave.astype(jnp.bfloat16)
        extended = with_halo(rounded, (("region", 1),), BND)
        picked = extended[:, local_col, :]
        current = jnp.einsum(
            "tbkj,bkij->tbi", picked, susceptance_maps, preferred_element_type=jnp.float32
        )
        drive = input_gain[None] * (drive_base - limit_current(current, saturated_flag[None]))
        local_a, local_b = lax.associative_scan(combine, (incremental_spin, drive), axis=0)
        own_map = (local_a[-1], local_b[-1])
        every_a, every_b = (
            lax.all_gather(own_map[0][None], "tm", axis=0, tiled=True),
            lax.all_gather(own_map[1][None], "tm", axis=0, tiled=True),
        )
        run_a, run_b = lax.associative_scan(combine, (every_a, every_b), axis=0)
        total_a, total_b = (run_a[-1], run_b[-1])
        time_index = lax.axis_index("tm")
        earlier = jnp.maximum(time_index - 1, 0)
        prior_a = lax.dynamic_index_in_dim(run_a, earlier, 0, keepdims=False)
        prior_b = lax.dynamic_index_in_dim(run_b, earlier, 0, keepdims=False)
        before = (
            jnp.where(time_index > 0, prior_a, unit),
            jnp.where(time_index > 0, prior_b, nothing),
        )
        end_state = periodic_end(total_a, total_b)
        start_state = complex_mul(before[0], end_state) + before[1]
        wave = complex_mul(local_a, start_state[None]) + local_b
    return wave


def solution(mesh):
    in_specs = (
        P(("cases", "tm"), "region", None),
        P(("cases", "tm"), "region", None),
        P("region", None, None, None),
        P("region", None),
        P("region", None),
        P("region", None),
        P(("cases", "region"), None),
        P(("cases", "tm")),
    )
    out_specs = P(("cases", "tm"), "region", None)
    return jax.shard_map(local, mesh=mesh, in_specs=in_specs, out_specs=out_specs, check_vma=False)
```

profile of v0, /device:TPU:0, one launch (start us, length us, event | category | flops | bytes accessed | tf_op | source)
XLA Modules:
  0.0 90.0 jit_solution(5454847663768018754)
XLA Ops:
  0.0 1.1 %copy.114 = bf16[48,8,128]{2,0,1:T(8,128)(2,1)S(1)} copy(f32[48,8,128]{2,1,0:T(8,128)} %param.8) | data formatting | bytes 294912 | tf_op args[0]
  1.1 0.5 collective-permute-start
  1.6 2.0 %collective-permute-start.1 = (bf16[48,4,128]{2,0,1:T(8,128)(2,1)S(1)}, bf16[48,4,128]{2,0,1:T(8,128)(2,1)S(1)}, u32[]{:S(2)}, u32[]{:S(2)}) collective-permute-start(bf16[48,4,128]{2,0,1:T(8,128)(2,1)S(1)} %get-tuple-element.68), channel_id=1, source_target_pairs={{1,0},{2,1},{3,2},{0,3},{5,4},{6,5},{7,6},{4,7},{9,8},{10,9},{11,1... | collective-permute-start | bytes 147464 | tf_op jit(solution)/shard_map/ppermute | solution.py:20
  3.6 0.7 copy-done.9
  4.5 0.5 copy-done.5
  5.1 0.7 copy-done.10
  5.9 0.6 copy-done.1
  6.6 0.6 gather_fusion
  8.0 0.7 copy-done.2
  12.4 0.5 slice-done
  13.4 14.1 %all_gather.14 = f32[4,8,128]{2,1,0:T(8,128)S(1)} all-gather(f32[1,8,128]{2,1,0:T(8,128)S(1)} %slice_add_fusion.40), channel_id=1, replica_groups=mesh['cases'=2,'tm'=4,'region'=4] {'tm'}, dimensions={0}, use_global_device_ids=true | all-gather | bytes 20480 | tf_op jit(solution)/shard_map/all_gather | solution.py:101
  28.5 13.1 %all_gather.15 = f32[4,8,128]{2,1,0:T(8,128)S(1)} all-gather(f32[1,8,128]{2,1,0:T(8,128)S(1)} %slice_add_fusion.37), channel_id=1, replica_groups=mesh['cases'=2,'tm'=4,'region'=4] {'tm'}, dimensions={0}, use_global_device_ids=true | all-gather | bytes 20480 | tf_op jit(solution)/shard_map/all_gather | solution.py:102
  42.3 0.7 slice-done.1
  43.0 0.7 copy-done.7
  44.5 1.7 %collective-permute-start.3 = (bf16[48,4,128]{2,1,0:T(4,128)(2,1)S(1)}, bf16[48,4,128]{2,1,0:T(4,128)(2,1)S(1)}, u32[]{:S(2)}, u32[]{:S(2)}) collective-permute-start(bf16[48,4,128]{2,1,0:T(4,128)(2,1)S(1)} %get-tuple-element.62), channel_id=1, source_target_pairs={{1,0},{2,1},{3,2},{0,3},{5,4},{6,5},{7,6},{4,7},{9,8},{10,9},{11,1... | collective-permute-start | bytes 147464 | tf_op jit(solution)/shard_map/ppermute | solution.py:20
  46.2 1.8 %collective-permute-done.2 = bf16[48,4,128]{2,1,0:T(4,128)(2,1)S(1)} collective-permute-done((bf16[48,4,128]{2,1,0:T(4,128)(2,1)S(1)}, bf16[48,4,128]{2,1,0:T(4,128)(2,1)S(1)}, u32[]{:S(2)}, u32[]{:S(2)}) %collective-permute-start.2) | collective-permute-done | bytes 49184 | tf_op jit(solution)/shard_map/ppermute | solution.py:17
  48.2 0.6 gather_fusion.1
  52.4 13.1 %all_gather.16 = f32[4,8,128]{2,1,0:T(8,128)S(1)} all-gather(f32[1,8,128]{2,1,0:T(8,128)S(1)} %slice_add_fusion.32), channel_id=1, replica_groups=mesh['cases'=2,'tm'=4,'region'=4] {'tm'}, dimensions={0}, use_global_device_ids=true | all-gather | bytes 20480 | tf_op jit(solution)/shard_map/all_gather | solution.py:102
  65.8 0.6 copy-done.4
  67.3 1.7 %collective-permute-start.5 = (bf16[48,4,128]{2,1,0:T(4,128)(2,1)S(1)}, bf16[48,4,128]{2,1,0:T(4,128)(2,1)S(1)}, u32[]{:S(2)}, u32[]{:S(2)}) collective-permute-start(bf16[48,4,128]{2,1,0:T(4,128)(2,1)S(1)} %get-tuple-element.58), channel_id=1, source_target_pairs={{1,0},{2,1},{3,2},{0,3},{5,4},{6,5},{7,6},{4,7},{9,8},{10,9},{11,1... | collective-permute-start | bytes 147464 | tf_op jit(solution)/shard_map/ppermute | solution.py:20
  69.0 1.8 %collective-permute-done.4 = bf16[48,4,128]{2,1,0:T(4,128)(2,1)S(1)} collective-permute-done((bf16[48,4,128]{2,1,0:T(4,128)(2,1)S(1)}, bf16[48,4,128]{2,1,0:T(4,128)(2,1)S(1)}, u32[]{:S(2)}, u32[]{:S(2)}) %collective-permute-start.4) | collective-permute-done | bytes 49184 | tf_op jit(solution)/shard_map/ppermute | solution.py:17
  70.9 0.6 gather_fusion.2
  75.2 13.1 %all_gather.17 = f32[4,8,128]{2,1,0:T(8,128)S(1)} all-gather(f32[1,8,128]{2,1,0:T(8,128)S(1)} %slice_add_fusion.27), channel_id=1, replica_groups=mesh['cases'=2,'tm'=4,'region'=4] {'tm'}, dimensions={0}, use_global_device_ids=true | all-gather | bytes 20480 | tf_op jit(solution)/shard_map/all_gather | solution.py:102
  89.2 0.8 maximum_add_fusion.2
  (290 shorter events, 16.2 us)
Async XLA Ops:
  0.0 7.3 %copy-start = (bf16[8,4,128,128]{3,2,1,0:T(8,128)(2,1)S(1)}, bf16[8,4,128,128]{3,2,1,0:T(8,128)(2,1)}, u32[]{:S(2)}) copy-start(bf16[8,4,128,128]{3,2,1,0:T(8,128)(2,1)} %param.10) | copy-start | bytes 3145732
  1.1 2.5 %copy-start.8 = (s32[8,64]{1,0:T(8,128)S(1)}, s32[8,64]{1,0:T(8,128)}, u32[]{:S(2)}) copy-start(s32[8,64]{1,0:T(8,128)} %param.14) | copy-start | bytes 6148
  1.1 5.5 %collective-permute-start = (bf16[48,4,128]{2,0,1:T(8,128)(2,1)S(1)}, bf16[48,4,128]{2,0,1:T(8,128)(2,1)S(1)}, u32[]{:S(2)}, u32[]{:S(2)}) collective-permute-start(bf16[48,4,128]{2,0,1:T(8,128)(2,1)S(1)} %get-tuple-element.67), channel_id=1, source_target_pairs={{0,1},{1,2},{2,3},{3,0},{4,5},{5,6},{6,7},{7,4},{8,9},{9,10},{10,1... | collective-permute-start | bytes 147464 | tf_op jit(solution)/shard_map/ppermute | solution.py:17
  1.6 5.0 %collective-permute-start.1 = (bf16[48,4,128]{2,0,1:T(8,128)(2,1)S(1)}, bf16[48,4,128]{2,0,1:T(8,128)(2,1)S(1)}, u32[]{:S(2)}, u32[]{:S(2)}) collective-permute-start(bf16[48,4,128]{2,0,1:T(8,128)(2,1)S(1)} %get-tuple-element.68), channel_id=1, source_target_pairs={{1,0},{2,1},{3,2},{0,3},{5,4},{6,5},{7,6},{4,7},{9,8},{10,9},{11,1... | collective-permute-start | bytes 147464 | tf_op jit(solution)/shard_map/ppermute | solution.py:20
  3.6 0.7 copy-start.9
  4.3 0.7 copy-start.5
  4.3 0.7 copy-start.6
  5.1 0.7 copy-start.10
  5.9 0.7 copy-start.1
  7.8 0.9 copy-start.2
  12.2 0.7 slice-start
  27.5 14.5 %copy-start.3 = (f32[4,8,128]{2,1,0:T(8,128)}, f32[4,8,128]{2,1,0:T(8,128)S(1)}, u32[]{:S(2)}) copy-start(f32[4,8,128]{2,1,0:T(8,128)S(1)} %all_gather.14) | copy-start | bytes 49156
  42.3 0.7 slice-start.1
  43.0 0.7 copy-start.7
  44.4 3.6 %collective-permute-start.2 = (bf16[48,4,128]{2,1,0:T(4,128)(2,1)S(1)}, bf16[48,4,128]{2,1,0:T(4,128)(2,1)S(1)}, u32[]{:S(2)}, u32[]{:S(2)}) collective-permute-start(bf16[48,4,128]{2,1,0:T(4,128)(2,1)S(1)} %get-tuple-element.61), channel_id=1, source_target_pairs={{0,1},{1,2},{2,3},{3,0},{4,5},{5,6},{6,7},{7,4},{8,9},{9,10},{10,1... | collective-permute-start | bytes 147464 | tf_op jit(solution)/shard_map/ppermute | solution.py:17
  44.5 3.5 %collective-permute-start.3 = (bf16[48,4,128]{2,1,0:T(4,128)(2,1)S(1)}, bf16[48,4,128]{2,1,0:T(4,128)(2,1)S(1)}, u32[]{:S(2)}, u32[]{:S(2)}) collective-permute-start(bf16[48,4,128]{2,1,0:T(4,128)(2,1)S(1)} %get-tuple-element.62), channel_id=1, source_target_pairs={{1,0},{2,1},{3,2},{0,3},{5,4},{6,5},{7,6},{4,7},{9,8},{10,9},{11,1... | collective-permute-start | bytes 147464 | tf_op jit(solution)/shard_map/ppermute | solution.py:20
  65.7 0.7 copy-start.4
  67.2 3.6 %collective-permute-start.4 = (bf16[48,4,128]{2,1,0:T(4,128)(2,1)S(1)}, bf16[48,4,128]{2,1,0:T(4,128)(2,1)S(1)}, u32[]{:S(2)}, u32[]{:S(2)}) collective-permute-start(bf16[48,4,128]{2,1,0:T(4,128)(2,1)S(1)} %get-tuple-element.57), channel_id=1, source_target_pairs={{0,1},{1,2},{2,3},{3,0},{4,5},{5,6},{6,7},{7,4},{8,9},{9,10},{10,1... | collective-permute-start | bytes 147464 | tf_op jit(solution)/shard_map/ppermute | solution.py:17
  67.3 3.5 %collective-permute-start.5 = (bf16[48,4,128]{2,1,0:T(4,128)(2,1)S(1)}, bf16[48,4,128]{2,1,0:T(4,128)(2,1)S(1)}, u32[]{:S(2)}, u32[]{:S(2)}) collective-permute-start(bf16[48,4,128]{2,1,0:T(4,128)(2,1)S(1)} %get-tuple-element.58), channel_id=1, source_target_pairs={{1,0},{2,1},{3,2},{0,3},{5,4},{6,5},{7,6},{4,7},{9,8},{10,9},{11,1... | collective-permute-start | bytes 147464 | tf_op jit(solution)/shard_map/ppermute | solution.py:20
where the time goes:
time: 90.4 us; the launch traced here: 90 us
  blocking collectives  53.5 us (59%)
  local copies, waits for them, and re-layouts  12.5 us (14%)
  other arithmetic  11.7 us (13%)
  starting transfers between devices  6.07 us (7%)
  waiting for transfers between devices  3.55 us (4%)
  matrix products  1.36 us (2%)
  between operations  1.28 us (1%)
    all_gather x3, blocking collectives, local(): lax.all_gather(own_map[1][None], 'tm', axis=0, tiled=True)  39.4 us
    all_gather x1, blocking collectives, local(): lax.all_gather(own_map[0][None], 'tm', axis=0, tiled=True)  14.1 us
    unnamed x26, local copies, waits for them, and re-layouts  5.99 us
    ppermute x3, starting transfers between devices, with_halo(): lax.ppermute(lax.slice_in_dim(block, 0, width, axis=dim), axis, backward)  5.45 us
    sub x45, other arithmetic, complex_mul(): first_re * second_re - first_im * second_im  4.13 us
    ppermute x3, waiting for transfers between devices, with_halo(): lax.ppermute(lax.slice_in_dim(block, block.shape[dim] - width, None, axis...  3.54 us
    add x33, other arithmetic, combine(): complex_mul(late[0], early[1]) + late[1]  2.7 us
    pad x34, local copies, waits for them, and re-layouts, local(): lax.associative_scan(combine, (incremental_spin, drive), axis=0)  2.34 us
  transfers between devices with their start and end apart: 6, of which 2 were waited for; matrix products, arithmetic and copies ran while one was open for 0% of the time, Pallas kernels for 0%

commit v1 on v0

--- a/solution.py
+++ b/solution.py
@@ -6,6 +6,18 @@
 BND = 4
 SWEEPS = 3
 clip_level = 0.5
+
+
+def doubled_up(x, axis, dim):
+    ways, here = (lax.axis_size(axis), lax.axis_index(axis))
+    grown, reach = (x, 1)
+    while reach < ways:
+        theirs = lax.ppermute(grown, axis, [(d, d ^ reach) for d in range(ways)])
+        mine_first = jnp.concatenate([grown, theirs], axis=dim)
+        theirs_first = jnp.concatenate([theirs, grown], axis=dim)
+        grown = jnp.where(here & reach == 0, mine_first, theirs_first)
+        reach = 2 * reach
+    return grown
 
 
 def with_halo(block, sides, width):
@@ -99,7 +111,7 @@
         own_map = (local_a[-1], local_b[-1])
         every_a, every_b = (
             lax.all_gather(own_map[0][None], "tm", axis=0, tiled=True),
-            lax.all_gather(own_map[1][None], "tm", axis=0, tiled=True),
+            doubled_up(own_map[1][None], "tm", 0),
         )
         run_a, run_b = lax.associative_scan(combine, (every_a, every_b), axis=0)
         total_a, total_b = (run_a[-1], run_b[-1])

time: 90.4 us -> 73.7 us (0.82)
  blocking collectives: 53.5 us -> 13.3 us
  waiting for transfers between devices: 3.55 us -> 21.4 us
  starting transfers between devices: 6.07 us -> 11.7 us
    all_gather x3 -> x0, blocking collectives: 39.4 us -> none  [local(): lax.all_gather(own_map[1][None], 'tm', axis=0, tiled=True)]
    ppermute x0 -> x6, waiting for transfers between devices: none -> 17.8 us  [doubled_up(): theirs = lax.ppermute(grown, axis, [(d, d ^ reach) for d in range(ways)])]
    ppermute x0 -> x6, starting transfers between devices: none -> 5.64 us  [doubled_up(): theirs = lax.ppermute(grown, axis, [(d, d ^ reach) for d in range(ways)])]
  transfers between devices with their start and end apart: 6 -> 12, of which waited for: 2 -> 7; matrix products, arithmetic and copies ran while one was open for 0% -> 1% of each run, Pallas kernels for 0% -> 0%
where the time goes in v1:
time: 73.7 us; the launch traced here: 73.3 us
  waiting for transfers between devices  21.4 us (29%)
  blocking collectives  13.3 us (18%)
  local copies, waits for them, and re-layouts  12.5 us (17%)
  other arithmetic  11.8 us (16%)
  starting transfers between devices  11.7 us (16%)
  matrix products  1.36 us (2%)
  between operations  1.28 us (2%)
    ppermute x6, waiting for transfers between devices, doubled_up(): theirs = lax.ppermute(grown, axis, [(d, d ^ reach) for d in range(ways)])  17.8 us
    all_gather x1, blocking collectives, local(): lax.all_gather(own_map[0][None], 'tm', axis=0, tiled=True)  13.3 us
    unnamed x26, local copies, waits for them, and re-layouts  5.99 us
    ppermute x6, starting transfers between devices, doubled_up(): theirs = lax.ppermute(grown, axis, [(d, d ^ reach) for d in range(ways)])  5.64 us
    ppermute x3, starting transfers between devices, with_halo(): lax.ppermute(lax.slice_in_dim(block, 0, width, axis=dim), axis, backward)  5.45 us
    sub x45, other arithmetic, complex_mul(): first_re * second_re - first_im * second_im  4.14 us
    ppermute x3, waiting for transfers between devices, with_halo(): lax.ppermute(lax.slice_in_dim(block, block.shape[dim] - width, None, axis...  3.54 us
    add x33, other arithmetic, combine(): complex_mul(late[0], early[1]) + late[1]  2.7 us
  transfers between devices with their start and end apart: 12, of which 7 were waited for; matrix products, arithmetic and copies ran while one was open for 1% of the time, Pallas kernels for 0%

profile of v1, /device:TPU:0, one launch (start us, length us, event | category | flops | bytes accessed | tf_op | source)
XLA Modules:
  0.0 73.3 jit_solution(3225129051459931420)
XLA Ops:
  0.0 1.1 %copy.147 = bf16[48,8,128]{2,0,1:T(8,128)(2,1)S(1)} copy(f32[48,8,128]{2,1,0:T(8,128)} %param.8) | data formatting | bytes 294912 | tf_op args[0]
  1.6 2.0 %collective-permute-start.1 = (bf16[48,4,128]{2,0,1:T(8,128)(2,1)S(1)}, bf16[48,4,128]{2,0,1:T(8,128)(2,1)S(1)}, u32[]{:S(2)}, u32[]{:S(2)}) collective-permute-start(bf16[48,4,128]{2,0,1:T(8,128)(2,1)S(1)} %get-tuple-element.68), channel_id=1, source_target_pairs={{1,0},{2,1},{3,2},{0,3},{5,4},{6,5},{7,6},{4,7},{9,8},{10,9},{11,1... | collective-permute-start | bytes 147464 | tf_op jit(solution)/shard_map/ppermute | solution.py:32
  3.6 0.7 copy-done.9
  5.1 0.7 copy-done.10
  5.9 0.6 copy-done.1
  8.0 0.7 %copy-done.2 = bf16[48,8,128]{2,1,0:T(8,128)(2,1)S(1)} copy-done((bf16[48,8,128]{2,1,0:T(8,128)(2,1)S(1)}, bf16[48,8,128]{2,1,0:T(8,128)(2,1)}, u32[]{:S(2)}) %copy-start.2) | copy-done | bytes 98328
  14.4 2.4 %collective-permute-start.2 = (f32[1,8,128]{2,1,0:T(8,128)S(1)}, f32[1,8,128]{2,1,0:T(8,128)S(1)}, u32[]{:S(2)}, u32[]{:S(2)}) collective-permute-start(f32[1,8,128]{2,1,0:T(8,128)S(1)} %slice_add_fusion.37), channel_id=1, source_target_pairs={{0,4},{4,0},{8,12},{12,8},{1,5},{5,1},{9,13},{13,9},{2,6},{6,2},{1... | collective-permute-start | bytes 12296 | tf_op jit(solution)/shard_map/ppermute | solution.py:15
  16.8 13.3 %all_gather.2 = f32[4,8,128]{2,1,0:T(8,128)S(1)} all-gather(f32[1,8,128]{2,1,0:T(8,128)S(1)} %slice_add_fusion.40), channel_id=1, replica_groups=mesh['cases'=2,'tm'=4,'region'=4] {'tm'}, dimensions={0}, use_global_device_ids=true | all-gather | bytes 20480 | tf_op jit(solution)/shard_map/all_gather | solution.py:113
  30.1 0.6 collective-permute-start.3
  30.8 4.0 %collective-permute-done.3 = f32[2,8,128]{2,1,0:T(8,128)S(1)} collective-permute-done((f32[2,8,128]{2,1,0:T(8,128)S(1)}, f32[2,8,128]{2,1,0:T(8,128)S(1)}, u32[]{:S(2)}, u32[]{:S(2)}) %collective-permute-start.3) | collective-permute-done | bytes 8224 | tf_op jit(solution)/shard_map/ppermute | solution.py:15
  35.4 0.7 slice-done.1
  36.2 0.7 copy-done.7
  37.6 1.7 %collective-permute-start.5 = (bf16[48,4,128]{2,1,0:T(4,128)(2,1)S(1)}, bf16[48,4,128]{2,1,0:T(4,128)(2,1)S(1)}, u32[]{:S(2)}, u32[]{:S(2)}) collective-permute-start(bf16[48,4,128]{2,1,0:T(4,128)(2,1)S(1)} %get-tuple-element.62), channel_id=1, source_target_pairs={{1,0},{2,1},{3,2},{0,3},{5,4},{6,5},{7,6},{4,7},{9,8},{10,9},{11,1... | collective-permute-start | bytes 147464 | tf_op jit(solution)/shard_map/ppermute | solution.py:32
  39.3 1.8 %collective-permute-done.4 = bf16[48,4,128]{2,1,0:T(4,128)(2,1)S(1)} collective-permute-done((bf16[48,4,128]{2,1,0:T(4,128)(2,1)S(1)}, bf16[48,4,128]{2,1,0:T(4,128)(2,1)S(1)}, u32[]{:S(2)}, u32[]{:S(2)}) %collective-permute-start.4) | collective-permute-done | bytes 49184 | tf_op jit(solution)/shard_map/ppermute | solution.py:29
  46.0 3.2 %collective-permute-done.6 = f32[1,8,128]{2,1,0:T(8,128)S(1)} collective-permute-done((f32[1,8,128]{2,1,0:T(8,128)S(1)}, f32[1,8,128]{2,1,0:T(8,128)S(1)}, u32[]{:S(2)}, u32[]{:S(2)}) %collective-permute-start.6) | collective-permute-done | bytes 4128 | tf_op jit(solution)/shard_map/ppermute | solution.py:15
  49.2 0.8 %collective-permute-start.7 = (f32[2,8,128]{2,1,0:T(8,128)S(1)}, f32[2,8,128]{2,1,0:T(8,128)S(1)}, u32[]{:S(2)}, u32[]{:S(2)}) collective-permute-start(f32[2,8,128]{2,1,0:T(8,128)S(1)} %maximum_select_fusion.4), channel_id=1, source_target_pairs={{0,8},{4,12},{8,0},{12,4},{1,9},{5,13},{9,1},{13,5},{2,10},{6,14},... | collective-permute-start | bytes 24584 | tf_op jit(solution)/shard_map/ppermute | solution.py:15
  50.0 3.8 %collective-permute-done.7 = f32[2,8,128]{2,1,0:T(8,128)S(1)} collective-permute-done((f32[2,8,128]{2,1,0:T(8,128)S(1)}, f32[2,8,128]{2,1,0:T(8,128)S(1)}, u32[]{:S(2)}, u32[]{:S(2)}) %collective-permute-start.7) | collective-permute-done | bytes 8224 | tf_op jit(solution)/shard_map/ppermute | solution.py:15
  54.1 0.6 copy-done.4
  55.5 1.7 %collective-permute-start.9 = (bf16[48,4,128]{2,1,0:T(4,128)(2,1)S(1)}, bf16[48,4,128]{2,1,0:T(4,128)(2,1)S(1)}, u32[]{:S(2)}, u32[]{:S(2)}) collective-permute-start(bf16[48,4,128]{2,1,0:T(4,128)(2,1)S(1)} %get-tuple-element.58), channel_id=1, source_target_pairs={{1,0},{2,1},{3,2},{0,3},{5,4},{6,5},{7,6},{4,7},{9,8},{10,9},{11,1... | collective-permute-start | bytes 147464 | tf_op jit(solution)/shard_map/ppermute | solution.py:32
  57.2 1.8 %collective-permute-done.8 = bf16[48,4,128]{2,1,0:T(4,128)(2,1)S(1)} collective-permute-done((bf16[48,4,128]{2,1,0:T(4,128)(2,1)S(1)}, bf16[48,4,128]{2,1,0:T(4,128)(2,1)S(1)}, u32[]{:S(2)}, u32[]{:S(2)}) %collective-permute-start.8) | collective-permute-done | bytes 49184 | tf_op jit(solution)/shard_map/ppermute | solution.py:29
  63.9 3.2 %collective-permute-done.10 = f32[1,8,128]{2,1,0:T(8,128)S(1)} collective-permute-done((f32[1,8,128]{2,1,0:T(8,128)S(1)}, f32[1,8,128]{2,1,0:T(8,128)S(1)}, u32[]{:S(2)}, u32[]{:S(2)}) %collective-permute-start.10) | collective-permute-done | bytes 4128 | tf_op jit(solution)/shard_map/ppermute | solution.py:15
  67.1 0.8 %collective-permute-start.11 = (f32[2,8,128]{2,1,0:T(8,128)S(1)}, f32[2,8,128]{2,1,0:T(8,128)S(1)}, u32[]{:S(2)}, u32[]{:S(2)}) collective-permute-start(f32[2,8,128]{2,1,0:T(8,128)S(1)} %maximum_select_fusion.5), channel_id=1, source_target_pairs={{0,8},{4,12},{8,0},{12,4},{1,9},{5,13},{9,1},{13,5},{2,10},{6,14},... | collective-permute-start | bytes 24584 | tf_op jit(solution)/shard_map/ppermute | solution.py:15
  67.9 3.8 %collective-permute-done.11 = f32[2,8,128]{2,1,0:T(8,128)S(1)} collective-permute-done((f32[2,8,128]{2,1,0:T(8,128)S(1)}, f32[2,8,128]{2,1,0:T(8,128)S(1)}, u32[]{:S(2)}, u32[]{:S(2)}) %collective-permute-start.11) | collective-permute-done | bytes 8224 | tf_op jit(solution)/shard_map/ppermute | solution.py:15
  72.5 0.8 %maximum_add_fusion.2 = f32[48,8,128]{2,1,0:T(8,128)} fusion(f32[48,8,64]{2,1,0:T(8,128)S(1)} %get-tuple-element.26, f32[48,8,64]{2,1,0:T(8,128)S(1)} %get-tuple-element.25, f32[48,8,128]{2,1,0:T(8,128)S(1)} %pad.254, f32[48,8,128]{2,1,0:T(8,128)S(1)} %pad.255), kind=kLoop, calls=%fused_computation.44 | loop fusion | flops 147456 | bytes 786432 | tf_op jit(solution)/shard_map/add | solution.py:128
  (305 shorter events, 20.7 us)
Async XLA Ops:
  0.0 7.3 %copy-start = (bf16[8,4,128,128]{3,2,1,0:T(8,128)(2,1)S(1)}, bf16[8,4,128,128]{3,2,1,0:T(8,128)(2,1)}, u32[]{:S(2)}) copy-start(bf16[8,4,128,128]{3,2,1,0:T(8,128)(2,1)} %param.10) | copy-start | bytes 3145732
  1.1 2.5 %copy-start.8 = (s32[8,64]{1,0:T(8,128)S(1)}, s32[8,64]{1,0:T(8,128)}, u32[]{:S(2)}) copy-start(s32[8,64]{1,0:T(8,128)} %param.14) | copy-start | bytes 6148
  1.1 5.5 %collective-permute-start = (bf16[48,4,128]{2,0,1:T(8,128)(2,1)S(1)}, bf16[48,4,128]{2,0,1:T(8,128)(2,1)S(1)}, u32[]{:S(2)}, u32[]{:S(2)}) collective-permute-start(bf16[48,4,128]{2,0,1:T(8,128)(2,1)S(1)} %get-tuple-element.67), channel_id=1, source_target_pairs={{0,1},{1,2},{2,3},{3,0},{4,5},{5,6},{6,7},{7,4},{8,9},{9,10},{10,1... | collective-permute-start | bytes 147464 | tf_op jit(solution)/shard_map/ppermute | solution.py:29
  1.6 5.0 %collective-permute-start.1 = (bf16[48,4,128]{2,0,1:T(8,128)(2,1)S(1)}, bf16[48,4,128]{2,0,1:T(8,128)(2,1)S(1)}, u32[]{:S(2)}, u32[]{:S(2)}) collective-permute-start(bf16[48,4,128]{2,0,1:T(8,128)(2,1)S(1)} %get-tuple-element.68), channel_id=1, source_target_pairs={{1,0},{2,1},{3,2},{0,3},{5,4},{6,5},{7,6},{4,7},{9,8},{10,9},{11,1... | collective-permute-start | bytes 147464 | tf_op jit(solution)/shard_map/ppermute | solution.py:32
  3.6 0.7 copy-start.9
  4.3 0.7 copy-start.5
  4.3 0.7 copy-start.6
  5.9 0.7 copy-start.1
  7.8 0.9 %copy-start.2 = (bf16[48,8,128]{2,1,0:T(8,128)(2,1)S(1)}, bf16[48,8,128]{2,1,0:T(8,128)(2,1)}, u32[]{:S(2)}) copy-start(bf16[48,8,128]{2,1,0:T(8,128)(2,1)} %param.9) | copy-start | bytes 294916
  12.7 0.7 slice-start
  14.4 15.7 %collective-permute-start.2 = (f32[1,8,128]{2,1,0:T(8,128)S(1)}, f32[1,8,128]{2,1,0:T(8,128)S(1)}, u32[]{:S(2)}, u32[]{:S(2)}) collective-permute-start(f32[1,8,128]{2,1,0:T(8,128)S(1)} %slice_add_fusion.37), channel_id=1, source_target_pairs={{0,4},{4,0},{8,12},{12,8},{1,5},{5,1},{9,13},{13,9},{2,6},{6,2},{1... | collective-permute-start | bytes 12296 | tf_op jit(solution)/shard_map/ppermute | solution.py:15
  30.1 5.0 %copy-start.3 = (f32[4,8,128]{2,1,0:T(8,128)}, f32[4,8,128]{2,1,0:T(8,128)S(1)}, u32[]{:S(2)}) copy-start(f32[4,8,128]{2,1,0:T(8,128)S(1)} %all_gather.2) | copy-start | bytes 49156
  30.1 4.6 %collective-permute-start.3 = (f32[2,8,128]{2,1,0:T(8,128)S(1)}, f32[2,8,128]{2,1,0:T(8,128)S(1)}, u32[]{:S(2)}, u32[]{:S(2)}) collective-permute-start(f32[2,8,128]{2,1,0:T(8,128)S(1)} %maximum_select_fusion.3), channel_id=1, source_target_pairs={{0,8},{4,12},{8,0},{12,4},{1,9},{5,13},{9,1},{13,5},{2,10},{6,14},... | collective-permute-start | bytes 24584 | tf_op jit(solution)/shard_map/ppermute | solution.py:15
  35.4 0.7 slice-start.1
  36.2 0.7 copy-start.7
  37.5 3.6 %collective-permute-start.4 = (bf16[48,4,128]{2,1,0:T(4,128)(2,1)S(1)}, bf16[48,4,128]{2,1,0:T(4,128)(2,1)S(1)}, u32[]{:S(2)}, u32[]{:S(2)}) collective-permute-start(bf16[48,4,128]{2,1,0:T(4,128)(2,1)S(1)} %get-tuple-element.61), channel_id=1, source_target_pairs={{0,1},{1,2},{2,3},{3,0},{4,5},{5,6},{6,7},{7,4},{8,9},{9,10},{10,1... | collective-permute-start | bytes 147464 | tf_op jit(solution)/shard_map/ppermute | solution.py:29
  37.6 3.5 %collective-permute-start.5 = (bf16[48,4,128]{2,1,0:T(4,128)(2,1)S(1)}, bf16[48,4,128]{2,1,0:T(4,128)(2,1)S(1)}, u32[]{:S(2)}, u32[]{:S(2)}) collective-permute-start(bf16[48,4,128]{2,1,0:T(4,128)(2,1)S(1)} %get-tuple-element.62), channel_id=1, source_target_pairs={{1,0},{2,1},{3,2},{0,3},{5,4},{6,5},{7,6},{4,7},{9,8},{10,9},{11,1... | collective-permute-start | bytes 147464 | tf_op jit(solution)/shard_map/ppermute | solution.py:32
  45.5 3.7 %collective-permute-start.6 = (f32[1,8,128]{2,1,0:T(8,128)S(1)}, f32[1,8,128]{2,1,0:T(8,128)S(1)}, u32[]{:S(2)}, u32[]{:S(2)}) collective-permute-start(f32[1,8,128]{2,1,0:T(8,128)S(1)} %slice_add_fusion.32), channel_id=1, source_target_pairs={{0,4},{4,0},{8,12},{12,8},{1,5},{5,1},{9,13},{13,9},{2,6},{6,2},{1... | collective-permute-start | bytes 12296 | tf_op jit(solution)/shard_map/ppermute | solution.py:15
  49.2 4.5 %collective-permute-start.7 = (f32[2,8,128]{2,1,0:T(8,128)S(1)}, f32[2,8,128]{2,1,0:T(8,128)S(1)}, u32[]{:S(2)}, u32[]{:S(2)}) collective-permute-start(f32[2,8,128]{2,1,0:T(8,128)S(1)} %maximum_select_fusion.4), channel_id=1, source_target_pairs={{0,8},{4,12},{8,0},{12,4},{1,9},{5,13},{9,1},{13,5},{2,10},{6,14},... | collective-permute-start | bytes 24584 | tf_op jit(solution)/shard_map/ppermute | solution.py:15
  54.0 0.7 copy-start.4
  55.4 3.6 %collective-permute-start.8 = (bf16[48,4,128]{2,1,0:T(4,128)(2,1)S(1)}, bf16[48,4,128]{2,1,0:T(4,128)(2,1)S(1)}, u32[]{:S(2)}, u32[]{:S(2)}) collective-permute-start(bf16[48,4,128]{2,1,0:T(4,128)(2,1)S(1)} %get-tuple-element.57), channel_id=1, source_target_pairs={{0,1},{1,2},{2,3},{3,0},{4,5},{5,6},{6,7},{7,4},{8,9},{9,10},{10,1... | collective-permute-start | bytes 147464 | tf_op jit(solution)/shard_map/ppermute | solution.py:29
  55.5 3.5 %collective-permute-start.9 = (bf16[48,4,128]{2,1,0:T(4,128)(2,1)S(1)}, bf16[48,4,128]{2,1,0:T(4,128)(2,1)S(1)}, u32[]{:S(2)}, u32[]{:S(2)}) collective-permute-start(bf16[48,4,128]{2,1,0:T(4,128)(2,1)S(1)} %get-tuple-element.58), channel_id=1, source_target_pairs={{1,0},{2,1},{3,2},{0,3},{5,4},{6,5},{7,6},{4,7},{9,8},{10,9},{11,1... | collective-permute-start | bytes 147464 | tf_op jit(solution)/shard_map/ppermute | solution.py:32
  63.4 3.7 %collective-permute-start.10 = (f32[1,8,128]{2,1,0:T(8,128)S(1)}, f32[1,8,128]{2,1,0:T(8,128)S(1)}, u32[]{:S(2)}, u32[]{:S(2)}) collective-permute-start(f32[1,8,128]{2,1,0:T(8,128)S(1)} %slice_add_fusion.27), channel_id=1, source_target_pairs={{0,4},{4,0},{8,12},{12,8},{1,5},{5,1},{9,13},{13,9},{2,6},{6,2},{1... | collective-permute-start | bytes 12296 | tf_op jit(solution)/shard_map/ppermute | solution.py:15
  67.1 4.5 %collective-permute-start.11 = (f32[2,8,128]{2,1,0:T(8,128)S(1)}, f32[2,8,128]{2,1,0:T(8,128)S(1)}, u32[]{:S(2)}, u32[]{:S(2)}) collective-permute-start(f32[2,8,128]{2,1,0:T(8,128)S(1)} %maximum_select_fusion.5), channel_id=1, source_target_pairs={{0,8},{4,12},{8,0},{12,4},{1,9},{5,13},{9,1},{13,5},{2,10},{6,14},... | collective-permute-start | bytes 24584 | tf_op jit(solution)/shard_map/ppermute | solution.py:15
  (1 other events, 0.7 us)
